TPU v7x, 32 devices: a whole 2x2x4 slice. The times are simulated.
32 devices in a mesh: grid: 2 (over x), mic: 4 (over z), bin: 4 (over y, core).
Axes of the slice: x: 2, y: 2, z: 4, core: 2. Of those that a mesh axis runs over, the one named last changes fastest.
Arguments:
- grid_points: float32 [3, 2048], P(None, 'grid'), may hold values from -1 to 3, as said below
- mic_coords: float32 [3, 4096], P(None, 'mic'), may hold values from -1 to 1, as said below
- wavenumbers: float32 [16], P('bin'), may hold values from 20 to 150
- pressures: float32 [16, 2, 16, 4096], P('bin', None, None, 'mic'), may hold values from -6 to 6
Outputs:
- solution: float32 [16, 2, 16, 2048], P('bin', None, None, 'grid')
- residual: float32 [16, 2, 16, 4096], P('bin', None, None, 'mic')
Inputs may be any that keep to these rules, and one draw needn't show every extreme that they name: `grid_points`: rows 0 and 1 lie in -1 to 1, row 2 in 1 to 3. `mic_coords`: rows 0 and 1 lie in -1 to 1, row 2 in -0.05 to 0.05.
All inputs are finite; a program needn't handle non-finite values.
Results may differ from a plain program's by a relative error of at most 0.0055.
Values may be sent and summed in bfloat16 or wider, within the bound.
A program may use at most 64 MiB of HBM per device.

v0:
```python
import math

import jax
import jax.numpy as jnp
from jax import lax
from jax.sharding import PartitionSpec as P

ITERS = 2


def steering_tiles(grid_points, mic_coords, wavenumbers, norm_scale):
    dist_x = grid_points[0][:, None] - mic_coords[0][None, :]
    dist_y = grid_points[1][:, None] - mic_coords[1][None, :]
    dist_z = grid_points[2][:, None] - mic_coords[2][None, :]
    radius = jnp.sqrt(dist_x * dist_x + dist_y * dist_y + dist_z * dist_z)
    amplitude = norm_scale / radius
    cos_list = []
    sin_list = []
    for bin_index in range(wavenumbers.shape[0]):
        phase_angle = wavenumbers[bin_index] * radius
        cos_list.append((jnp.cos(phase_angle) * amplitude).astype(jnp.bfloat16))
        sin_list.append((jnp.sin(phase_angle) * amplitude).astype(jnp.bfloat16))
    return (jnp.stack(cos_list), jnp.stack(sin_list))


def body(grid_points, mic_coords, wavenumbers, pressures):
    bin_count = pressures.shape[0]
    snap_count = pressures.shape[2]
    grid_local = grid_points.shape[1]
    norm_scale = 1.0 / math.sqrt(grid_local * lax.axis_size("grid"))
    cos_tiles, sin_tiles = steering_tiles(grid_points, mic_coords, wavenumbers, norm_scale)

    def combine_adjoint(cos_sum, sin_sum):
        real_part = cos_sum[:, :snap_count] - sin_sum[:, snap_count:]
        imag_part = cos_sum[:, snap_count:] + sin_sum[:, :snap_count]
        return jnp.stack([real_part, imag_part], axis=1)

    def apply_adjoint(residual):
        rounded = residual.astype(jnp.bfloat16).reshape(
            bin_count, 2 * snap_count, residual.shape[3]
        )
        cos_sum = jnp.einsum("fkm,fgm->fkg", rounded, cos_tiles, preferred_element_type=jnp.float32)
        sin_sum = jnp.einsum("fkm,fgm->fkg", rounded, sin_tiles, preferred_element_type=jnp.float32)
        partial_terms = combine_adjoint(cos_sum, sin_sum)
        summed = lax.psum(partial_terms, "mic")
        grad_norm = lax.psum(jnp.sum(summed * summed), ("grid", "bin"))
        return (summed, grad_norm)

    residual = pressures
    gradient, grad_norm = apply_adjoint(residual)
    direction = gradient
    solution = jnp.zeros_like(gradient)
    for iteration in range(ITERS):
        apply_rounded = direction.astype(jnp.bfloat16).reshape(
            bin_count, 2 * snap_count, direction.shape[3]
        )
        apply_cos_sum = jnp.einsum(
            "fkg,fgm->fkm", apply_rounded, cos_tiles, preferred_element_type=jnp.float32
        )
        apply_sin_sum = jnp.einsum(
            "fkg,fgm->fkm", apply_rounded, sin_tiles, preferred_element_type=jnp.float32
        )
        combine_real_part = apply_cos_sum[:, :snap_count] + apply_sin_sum[:, snap_count:]
        combine_imag_part = apply_cos_sum[:, snap_count:] - apply_sin_sum[:, :snap_count]
        apply_partial_terms = jnp.stack([combine_real_part, combine_imag_part], axis=1)
        apply_summed = lax.psum(apply_partial_terms, "grid")
        image_norm = lax.psum(jnp.sum(apply_summed * apply_summed), ("mic", "bin"))
        image, image_norm = (apply_summed, image_norm)
        step_size = grad_norm / image_norm
        solution = solution + step_size * direction
        residual = residual - step_size * image
        if iteration + 1 < ITERS:
            gradient, next_norm = apply_adjoint(residual)
            direction = gradient + next_norm / grad_norm * direction
            grad_norm = next_norm
    return (solution, residual)


def solution(mesh):
    placed = (P(None, "grid"), P(None, "mic"), P("bin"), P("bin", None, None, "mic"))
    return jax.shard_map(
        body,
        mesh=mesh,
        in_specs=placed,
        out_specs=(P("bin", None, None, "grid"), P("bin", None, None, "mic")),
        check_vma=False,
    )
```

profile of v0, /device:TPU:0, one launch (start us, length us, event | category | flops | bytes accessed | tf_op | source)
XLA Modules:
  0.0 370.2 jit_solution(3494871839418942299)
XLA Ops:
  7.2 0.0 all-reduce.5.cloned.1.call-start
  7.2 1.5 fusion.13
  8.7 0.8 fusion.11
  9.5 0.8 fusion.12
  10.4 1.1 convert_element_type.96
  11.5 67.4 %multiply_convert_fusion.7 = (bf16[1,1024,1024]{2,1,0:T(8,128)(2,1)S(1)}, bf16[1,1024,1024]{2,1,0:T(8,128)(2,1)S(1)}, bf16[1,1024,1024]{2,1,0:T(8,128)(2,1)S(1)}...) fusion(f32[1024]{0:T(1024)S(1)} %bitcast.62, ...), kind=kLoop, calls=%fused_computation.9 | loop fusion | flops 30408704 | bytes 16801808 | tf_op jit(solution)/shard_map/convert_element_type | solution.py:21
  78.9 2.4 pad_maximum_fusion
  81.3 2.6 convolution_bitcast_fusion
  83.9 0.6 copy-done
  84.5 2.5 copy-done.2
  87.0 2.6 convolution_bitcast_fusion.1
  89.6 0.1 fusion.8
  89.6 0.8 pad_maximum_fusion.2
  90.5 0.0 all-reduce.5.cloned.1.call-update
  90.5 0.0 all-reduce.7.cloned.1.call-start
  90.6 41.1 %all-reduce.5.cloned.1.call-done = f32[4,2,16,1024]{3,2,0,1:T(8,128)} async-done(((f32[4,2,16,1024]{3,2,0,1:T(8,128)}), f32[4,2,16,1024]{3,2,0,1:T(8,128)}) %all-reduce.5.cloned.1.call-update) | async-done | bytes 524304 | tf_op jit(solution)/shard_map/psum | solution.py:45
  131.6 1.9 multiply_reduce_fusion.3
  133.6 5.1 %fusion.14 = f32[4,32,1024]{2,1,0:T(8,128)S(1)} fusion(bf16[4,32,1024]{2,1,0:T(8,128)(2,1)S(1)} %bitcast.54, bf16[4,1024,1024]{2,1,0:T(8,128)(2,1)} %copy-done.2), kind=kOutput, calls=%fused_computation.47 | convolution fusion | flops 268435456 | bytes 9175040 | tf_op jit(solution)/shard_map/fkg,fgm->fkm/dot_general | solution.py:57
  138.7 0.7 copy-done.1
  139.4 1.5 fusion.15
  140.9 0.1 fusion.6
  141.0 0.8 pad_maximum_fusion.3
  141.8 0.0 all-reduce.9.cloned.1.call-start
  141.9 28.7 %all-reduce.7.cloned.1.call-done = f32[4,2,16,1024]{3,2,0,1:T(8,128)} async-done(((f32[4,2,16,1024]{3,2,0,1:T(8,128)}), f32[4,2,16,1024]{3,2,0,1:T(8,128)}) %all-reduce.7.cloned.1.call-update) | async-done | bytes 524304 | tf_op jit(solution)/shard_map/psum | solution.py:66
  170.6 1.8 multiply_reduce_fusion.2
  172.4 13.3 %psum.57 = f32[]{:T(128)} all-reduce(f32[]{:T(128)} %get-tuple-element.14), channel_id=1, replica_groups=mesh['grid'=2,'mic'=4,'bin'=4] {'grid','bin'}, use_global_device_ids=true, to_apply=%region_2.0 | all-reduce | flops 1 | bytes 8 | tf_op jit(solution)/shard_map/psum | solution.py:46
  185.7 32.3 %psum.59 = f32[]{:T(128)} all-reduce(f32[]{:T(128)} %multiply_reduce_fusion.2), channel_id=1, replica_groups=mesh['grid'=2,'mic'=4,'bin'=4] {'mic','bin'}, use_global_device_ids=true, to_apply=%region_5.0 | all-reduce | flops 1 | bytes 8 | tf_op jit(solution)/shard_map/psum | solution.py:67
  219.4 1.1 fusion.10
  220.5 6.0 %fusion.16 = f32[4,32,1024]{2,1,0:T(8,128)S(1)} fusion(bf16[4,32,1024]{2,1,0:T(8,128)(2,1)S(1)} %bitcast.56, bf16[4,1024,1024]{2,1,0:T(8,128)(2,1)} %copy-done.2), kind=kOutput, calls=%fused_computation.49 | convolution fusion | flops 268435456 | bytes 9175040 | tf_op jit(solution)/shard_map/fkm,fgm->fkg/dot_general | solution.py:42
  226.5 6.0 %fusion.17 = f32[4,32,1024]{2,1,0:T(8,128)S(1)} fusion(bf16[4,32,1024]{2,1,0:T(8,128)(2,1)S(1)} %bitcast.57, bf16[4,1024,1024]{2,1,0:T(8,128)(2,1)} %copy-done), kind=kOutput, calls=%fused_computation.50 | convolution fusion | flops 268435456 | bytes 9175040 | tf_op jit(solution)/shard_map/fkm,fgm->fkg/dot_general | solution.py:43
  232.5 0.1 fusion.4
  232.6 0.8 pad_maximum_fusion.4
  233.4 0.0 all-reduce.11.cloned.1.call-start
  233.5 34.7 %all-reduce.9.cloned.1.call-done = f32[4,2,16,1024]{3,2,0,1:T(8,128)} async-done(((f32[4,2,16,1024]{3,2,0,1:T(8,128)}), f32[4,2,16,1024]{3,2,0,1:T(8,128)}) %all-reduce.9.cloned.1.call-update) | async-done | bytes 524304 | tf_op jit(solution)/shard_map/psum | solution.py:45
  268.2 1.8 multiply_reduce_fusion.1
  270.0 13.6 %psum.61 = f32[]{:T(128)} all-reduce(f32[]{:T(128)} %multiply_reduce_fusion.1), channel_id=1, replica_groups=mesh['grid'=2,'mic'=4,'bin'=4] {'grid','bin'}, use_global_device_ids=true, to_apply=%region_8.0 | all-reduce | flops 1 | bytes 8 | tf_op jit(solution)/shard_map/psum | solution.py:46
  284.9 1.1 fusion.9
  286.0 4.9 %fusion.18 = f32[4,32,1024]{2,1,0:T(8,128)S(1)} fusion(bf16[4,32,1024]{2,1,0:T(8,128)(2,1)S(1)} %bitcast.52, bf16[4,1024,1024]{2,1,0:T(8,128)(2,1)} %copy-done.2), kind=kOutput, calls=%fused_computation.51 | convolution fusion | flops 268435456 | bytes 9175040 | tf_op jit(solution)/shard_map/fkg,fgm->fkm/dot_general | solution.py:57
  291.0 5.0 %fusion.19 = f32[4,32,1024]{2,1,0:T(8,128)S(1)} fusion(bf16[4,32,1024]{2,1,0:T(8,128)(2,1)S(1)} %bitcast.53, bf16[4,1024,1024]{2,1,0:T(8,128)(2,1)} %copy-done), kind=kOutput, calls=%fused_computation.52 | convolution fusion | flops 268435456 | bytes 9175040 | tf_op jit(solution)/shard_map/fkg,fgm->fkm/dot_general | solution.py:60
  296.0 0.1 fusion.2
  296.0 0.8 pad_maximum_fusion.5
  296.9 26.9 %all-reduce.11.cloned.1.call-done = f32[4,2,16,1024]{3,2,0,1:T(8,128)} async-done(((f32[4,2,16,1024]{3,2,0,1:T(8,128)}), f32[4,2,16,1024]{3,2,0,1:T(8,128)}) %all-reduce.11.cloned.1.call-update) | async-done | bytes 524304 | tf_op jit(solution)/shard_map/psum | solution.py:66
  323.8 1.8 multiply_reduce_fusion
  325.6 33.8 %psum.63 = f32[]{:T(128)} all-reduce(f32[]{:T(128)} %multiply_reduce_fusion), channel_id=1, replica_groups=mesh['grid'=2,'mic'=4,'bin'=4] {'mic','bin'}, use_global_device_ids=true, to_apply=%region_11.0 | all-reduce | flops 1 | bytes 8 | tf_op jit(solution)/shard_map/psum | solution.py:67
  360.7 1.2 multiply_subtract_fusion
  361.9 0.8 copy.14
  362.7 0.1 multiply_add_fusion
  362.8 0.8 copy.13
  (17 shorter events, 0.1 us)
Async XLA Ops:
  7.2 124.5 %all-reduce.5.cloned.1.call-start = ((), (), s32[]{:S(2)}) async-start(), calls=%async_computation | async-start | bytes 1048576 | tf_op jit(solution)/shard_map/psum | solution.py:45
  81.3 3.2 copy-start
  81.3 5.7 %copy-start.2 = (bf16[4,1024,1024]{2,1,0:T(8,128)(2,1)}, bf16[4,1024,1024]{2,1,0:T(8,128)(2,1)S(1)}, u32[]{:S(2)}) copy-start(bf16[4,1024,1024]{2,1,0:T(8,128)(2,1)S(1)} %get-tuple-element.34) | copy-start | bytes 25165828
  90.5 80.1 %all-reduce.7.cloned.1.call-start = ((), (), s32[]{:S(2)}) async-start(), calls=%async_computation.1 | async-start | bytes 1048576 | tf_op jit(solution)/shard_map/psum | solution.py:66
  133.6 5.8 %copy-start.1 = (bf16[4,1024,1024]{2,1,0:T(8,128)(2,1)S(1)}, bf16[4,1024,1024]{2,1,0:T(8,128)(2,1)}, u32[]{:S(2)}) copy-start(bf16[4,1024,1024]{2,1,0:T(8,128)(2,1)} %copy-done) | copy-start | bytes 25165828
  139.4 80.0 %copy-start.5 = (f32[4,2,16,1024]{3,2,1,0:T(8,128)S(1)}, f32[4,2,16,1024]{3,2,1,0:T(8,128)}, u32[]{:S(2)}) copy-start(f32[4,2,16,1024]{3,2,1,0:T(8,128)} %param.7) | copy-start | bytes 1572868
  141.8 126.3 %all-reduce.9.cloned.1.call-start = ((), (), s32[]{:S(2)}) async-start(), calls=%async_computation.2 | async-start | bytes 1048576 | tf_op jit(solution)/shard_map/psum | solution.py:45
  226.5 58.4 %copy-start.3 = (f32[4,2,16,1024]{3,2,0,1:T(8,128)S(1)}, f32[4,2,16,1024]{3,2,0,1:T(8,128)}, u32[]{:S(2)}) copy-start(f32[4,2,16,1024]{3,2,0,1:T(8,128)} %all-reduce.5.cloned.1.call-done) | copy-start | bytes 1572868
  233.4 90.4 %all-reduce.11.cloned.1.call-start = ((), (), s32[]{:S(2)}) async-start(), calls=%async_computation.3 | async-start | bytes 1048576 | tf_op jit(solution)/shard_map/psum | solution.py:66
  291.0 69.8 %copy-start.6 = (f32[4,2,16,1024]{3,2,0,1:T(8,128)S(1)}, f32[4,2,16,1024]{3,2,0,1:T(8,128)}, u32[]{:S(2)}) copy-start(f32[4,2,16,1024]{3,2,0,1:T(8,128)} %all-reduce.7.cloned.1.call-done) | copy-start | bytes 1572868
  296.0 66.8 %copy-start.4 = (f32[4,2,16,1024]{3,2,0,1:T(8,128)S(1)}, f32[4,2,16,1024]{3,2,0,1:T(8,128)}, u32[]{:S(2)}) copy-start(f32[4,2,16,1024]{3,2,0,1:T(8,128)} %all-reduce.9.cloned.1.call-done) | copy-start | bytes 1572868
Sparse Core Ops, SparseCore 0:
  90.6 40.9 all-reduce.4
  142.0 28.5 all-reduce.6
  233.5 34.6 all-reduce.8
  297.0 26.7 all-reduce.10
where the time goes:
time: 371 us; the launch traced here: 370 us
  waiting for transfers between devices  132 us (36%)
  blocking collectives  93 us (25%)
  other arithmetic  85.2 us (23%)
  matrix products  33.6 us (9%)
  between operations  17.9 us (5%)
  local copies, waits for them, and re-layouts  8.72 us (2%)
    psum x2, waiting for transfers between devices, apply_adjoint(): summed = lax.psum(partial_terms, 'mic')  75.8 us
    convert_element_type x1, other arithmetic, steering_tiles(): cos_list.append((jnp.cos(phase_angle) * amplitude).astype(jnp.bfloat16))  67.4 us
    psum x2, blocking collectives, body(): image_norm = lax.psum(jnp.sum(apply_summed * apply_summed), ('mic', 'bin'))  66.1 us
    psum x2, waiting for transfers between devices, body(): apply_summed = lax.psum(apply_partial_terms, 'grid')  55.6 us
    psum x2, blocking collectives, apply_adjoint(): grad_norm = lax.psum(jnp.sum(summed * summed), ('grid', 'bin'))  26.9 us
    dot_general x2, matrix products, body(): jnp.einsum('fkg,fgm->fkm', apply_rounded, cos_tiles, preferred_element_ty...  10 us
    dot_general x2, matrix products, apply_adjoint(): jnp.einsum('fkm,fgm->fkg', rounded, sin_tiles, preferred_element_type=jnp...  8.58 us
    dot_general x2, matrix products, apply_adjoint(): jnp.einsum('fkm,fgm->fkg', rounded, cos_tiles, preferred_element_type=jnp...  8.53 us
  transfers between devices with their start and end apart: 4, of which 4 were waited for; matrix products, arithmetic and copies ran while one was open for 0% of the time, Pallas kernels for 0%

commit v1 on v0

--- a/solution.py
+++ b/solution.py
@@ -1,9 +1,397 @@
+import functools
 import math
 
 import jax
 import jax.numpy as jnp
 from jax import lax
+from jax.experimental import pallas as pl
+from jax.experimental.pallas import tpu as pltpu
 from jax.sharding import PartitionSpec as P
+
+MESH = pl.DeviceIdType.MESH
+F32 = jnp.float32
+BF16 = jnp.bfloat16
+
+SIN_COEF = (4.4428679, -7.30744342, 3.59478804, -0.78437393)
+COS_COEF = (1.41420408, -6.97764205, 5.71523831, -1.72834838)
+ROUNDER = 12582912.0
+ROWS = 32
+BLOCK = 512
+
+
+def poly(coef, s):
+    total = coef[-1]
+    for value in coef[-2::-1]:
+        total = total * s + value
+    return total
+
+
+def kernel(norm_scale, gp_ref, mc_ref, wn_ref, p_ref, sol_ref, res_ref,
+           gp_all, mc_all, wn_buf, gcol, cos_t, sin_t, p_send, p_all, op_a, op_b,
+           part, part_in, grad, image, grad_half, image_half, sol_in, res_in,
+           red_out, red_in, red_y, red_y_in,
+           co_send, co_recv, p_ssem, p_rsem, ex_ssem, ex_rsem, so_ssem, so_rsem,
+           re_ssem, re_rsem, fw_ssem, rd_ssem, rd_rsem, ry_sem):
+    x, z, b = lax.axis_index("grid"), lax.axis_index("mic"), lax.axis_index("bin")
+    y, c = b // 2, b % 2
+    half = z // 2
+    n_mic = mc_ref.shape[1]
+    n_grid = gp_ref.shape[1]
+
+    def dev(gx, mz, core, plane=None):
+        plane = y if plane is None else plane
+        return {"grid": gx, "mic": mz, "bin": plane * 2 + core}
+
+    other_core = dev(x, z, 1 - c)
+
+    def rcopy(src, dst, ssem, rsem, device):
+        return pltpu.make_async_remote_copy(
+            src_ref=src, dst_ref=dst, send_sem=ssem, recv_sem=rsem, device_id=device, device_id_type=MESH)
+
+    offsets = [(dx, dz, dc) for dx in range(2) for dz in range(4) for dc in range(2)][1:]
+
+    def at_offset(o):
+        return dev((x + o[0]) % 2, (z + o[1]) % 4, (c + o[2]) % 2)
+
+    barrier = pltpu.get_barrier_semaphore()
+    for o in offsets:
+        pl.semaphore_signal(barrier, inc=1, device_id=at_offset(o), device_id_type=MESH)
+    pl.semaphore_signal(barrier, inc=1, device_id=dev(x, z, c, 1 - y), device_id_type=MESH)
+    pl.semaphore_wait(barrier, len(offsets) + 1)
+
+    gp_copy = rcopy(gp_ref, gp_all.at[x], co_send.at[0], co_recv.at[0], dev(1 - x, z, c))
+    gp_copy.start()
+
+    def mic_copy(shift):
+        return rcopy(mc_ref, mc_all.at[z % 2], co_send.at[1 + shift], co_recv.at[1 + z % 2],
+                     dev(x, (z + shift) % 4, c))
+
+    @pl.when(c == half)
+    def _():
+        for shift in range(1, 4):
+            mic_copy(shift).start()
+        mc_all[z % 2] = mc_ref[...]
+
+    wn_copy = rcopy(wn_buf, wn_buf, co_send.at[0 + 4], co_recv.at[3], other_core)
+
+    @pl.when(c == x)
+    def _():
+        wn_buf[...] = jnp.full(wn_buf.shape, wn_ref[z], F32)
+        wn_copy.start()
+
+    gp_all[x] = gp_ref[...]
+
+    def p_copy(shift):
+        to = (z + shift) % 4
+        return rcopy(p_send.at[to], p_all.at[z % 2], p_ssem.at[shift], p_rsem.at[z % 2], dev(x, to, half))
+
+    @pl.when(c == x)
+    def _():
+        p_send[...] = p_ref[...].astype(BF16)
+        for shift in range(4):
+            if shift:
+                p_copy(shift).start()
+            else:
+                @pl.when(c != half)
+                def _():
+                    p_copy(0).start()
+
+                @pl.when(c == half)
+                def _():
+                    p_all[z % 2] = p_send[z]
+
+    gp_copy.wait_recv()
+    for j in range(2):
+        @pl.when(z != 2 * c + j)
+        def _():
+            rcopy(mc_ref, mc_all.at[j], co_send.at[1], co_recv.at[1 + j], other_core).wait_recv()
+
+    @pl.when(c != x)
+    def _():
+        wn_copy.wait_recv()
+
+    turns = wn_buf[0:1, 0:1] * (1.0 / (2.0 * math.pi))
+    amp_scale = turns * norm_scale
+    gp_all[...] = gp_all[...] * turns[None]
+    mc_all[...] = mc_all[...] * turns[None]
+    for h in range(2):
+        for d in range(3):
+            for k in range(n_grid // 128):
+                row = gp_all[h, d:d + 1, k * 128:(k + 1) * 128]
+                gcol[d, h * n_grid + k * 128:h * n_grid + (k + 1) * 128, :] = jnp.broadcast_to(row, (128, 128)).T
+
+    scale_row = jnp.broadcast_to(amp_scale, (ROWS, 128))
+
+    @pl.loop(0, 2 * n_grid // ROWS)
+    def _(i):
+        rows = pl.ds(pl.multiple_of(i * ROWS, ROWS), ROWS)
+        gx, gy, gz = gcol[0, rows, :], gcol[1, rows, :], gcol[2, rows, :]
+        for j in range(2):
+            for k in range(n_mic // 128):
+                lanes = slice(k * 128, (k + 1) * 128)
+                dx = gx - mc_all[j, 0:1, lanes]
+                dy = gy - mc_all[j, 1:2, lanes]
+                dz = gz - mc_all[j, 2:3, lanes]
+                q = dx * dx + dy * dy + dz * dz
+                inv = lax.rsqrt(q)
+                t = q * inv
+                amp = inv * scale_row
+                f = t - ((t + ROUNDER) - ROUNDER)
+                s = f * f
+                sine = f * poly(SIN_COEF, s)
+                cosine = poly(COS_COEF, s)
+                scaled = sine * amp
+                cols = slice(j * n_mic + k * 128, j * n_mic + (k + 1) * 128)
+                cos_t[rows, cols] = (amp - scaled * sine).astype(BF16)
+                sin_t[rows, cols] = (scaled * cosine).astype(BF16)
+
+    for j in range(2):
+        @pl.when(jnp.logical_not(jnp.logical_and(z == 2 * c + j, c == x)))
+        def _():
+            rcopy(p_send.at[0], p_all.at[j], p_ssem.at[0], p_rsem.at[j], other_core).wait_recv()
+
+    def operands(blocks, adjoint):
+        for j in range(2):
+            v = blocks[j]
+            real, imag = v[:16], v[16:]
+            swapped = [-imag, real] if adjoint else [imag, -real]
+            cols = slice(j * v.shape[1], (j + 1) * v.shape[1])
+            op_a[:, cols] = v
+            op_b[:, cols] = jnp.concatenate(swapped, axis=0)
+
+    def products(accs, pairs):
+        out = []
+        for acc, (left, right) in zip(accs, pairs):
+            prod = left * right
+            out.append(acc + jnp.sum(prod.reshape(4, 8, prod.shape[1]), axis=0))
+        return out
+
+    def ex_copy(v, k):
+        cols = pl.ds(k * BLOCK, BLOCK)
+        return rcopy(part.at[v, :, cols], part_in.at[v, :, cols], ex_ssem.at[v, k], ex_rsem.at[v, k], other_core)
+
+    def adjoint(v):
+        for k in range(2 * n_grid // BLOCK):
+            rows = slice(k * BLOCK, (k + 1) * BLOCK)
+            dims = (((1,), (1,)), ((), ()))
+            part[v, :, rows] = (
+                lax.dot_general(op_a[...], cos_t[rows, :], dims, preferred_element_type=F32)
+                + lax.dot_general(op_b[...], sin_t[rows, :], dims, preferred_element_type=F32))
+            ex_copy(v, k).start()
+        for k in range(2 * n_grid // BLOCK):
+            cols = slice(k * BLOCK, (k + 1) * BLOCK)
+            ex_copy(v, k).wait_recv()
+            total = part[v, :, cols] + part_in[v, :, cols]
+            grad[v, :, cols] = total
+            h, low = divmod(k * BLOCK, n_grid)
+            grad_half[v, h, :, low:low + BLOCK] = total.astype(BF16)
+
+    def forward(v):
+        for k in range(2 * n_mic // BLOCK):
+            cols = slice(k * BLOCK, (k + 1) * BLOCK)
+            total = (jnp.dot(op_a[...], cos_t[:, cols], preferred_element_type=F32)
+                     + jnp.dot(op_b[...], sin_t[:, cols], preferred_element_type=F32))
+            image[v, :, cols] = total
+            h, low = divmod(k * BLOCK, n_mic)
+            image_half[v, h, :, low:low + BLOCK] = total.astype(BF16)
+
+    def sol_copy(v, shift):
+        to = (z + shift) % 4
+        return rcopy(grad_half.at[v, c], sol_in.at[v, z], so_ssem.at[v, shift], so_rsem.at[v, z], dev(c, to, x))
+
+    def send_sol(v):
+        for shift in range(1, 4):
+            sol_copy(v, shift).start()
+
+        @pl.when(c != x)
+        def _():
+            sol_copy(v, 0).start()
+
+        @pl.when(c == x)
+        def _():
+            sol_in[v, z] = grad_half[v, c]
+
+    def res_copy(v, j):
+        return rcopy(image_half.at[v, j], res_in.at[v, z], re_ssem.at[v, j], re_rsem.at[v, z], dev(x, 2 * c + j, x))
+
+    def own_quarter(j):
+        return jnp.logical_and(z == 2 * c + j, c == x)
+
+    def send_res(v):
+        for j in range(2):
+            @pl.when(jnp.logical_not(own_quarter(j)))
+            def _():
+                res_copy(v, j).start()
+
+            @pl.when(own_quarter(j))
+            def _():
+                res_in[v, z] = image_half[v, j]
+
+    def fw_copy(v, l):
+        return rcopy(res_in.at[v, l], res_in.at[v, l], fw_ssem.at[v, l], re_rsem.at[v, l], dev(1 - x, z, c))
+
+    def forward_res(v):
+        @pl.when(c == x)
+        def _():
+            for l in range(4):
+                @pl.when(jnp.logical_not(jnp.logical_and(z == l, c == half)))
+                def _():
+                    fw_copy(v, l).wait_recv()
+                fw_copy(v, l).start()
+
+    operands([p_all[0], p_all[1]], True)
+    adjoint(0)
+    send_sol(0)
+    operands([grad_half[0, 0], grad_half[0, 1]], False)
+    forward(0)
+    send_res(0)
+    operands([image_half[0, 0], image_half[0, 1]], True)
+    adjoint(1)
+    send_sol(1)
+    operands([grad_half[1, 0], grad_half[1, 1]], False)
+    forward(1)
+    send_res(1)
+    forward_res(0)
+
+    zero = jnp.zeros((8, 128), F32)
+    accs = [zero] * 6
+    for k in range(2 * n_grid // 128):
+        cols = slice(k * 128, (k + 1) * 128)
+        g, u = grad[0, :, cols], grad[1, :, cols]
+        accs[:3] = products(accs[:3], [(g, g), (g, u), (u, u)])
+    for k in range(2 * n_mic // 128):
+        cols = slice(k * 128, (k + 1) * 128)
+        q, w = image[0, :, cols], image[1, :, cols]
+        accs[3:] = products(accs[3:], [(q, q), (q, w), (w, w)])
+    for i in range(6):
+        weight = 0.5 if i < 3 else 1.0
+        red_out[i:i + 1, :] = weight * jnp.sum(accs[i], axis=0, keepdims=True)
+    red_out[6:8, :] = jnp.zeros((2, 128), F32)
+
+    me = (x * 4 + z) * 2 + c
+
+    def rd_copy(i):
+        return rcopy(red_out, red_in.at[me], rd_ssem.at[i], rd_rsem.at[i], at_offset(offsets[i]))
+
+    for i in range(len(offsets)):
+        rd_copy(i).start()
+    red_in[me] = red_out[...]
+    for i in range(len(offsets)):
+        rd_copy(i).wait_recv()
+    total = red_in[0]
+    for i in range(1, len(offsets) + 1):
+        total = total + red_in[i]
+    red_y[...] = total
+    y_copy = rcopy(red_y, red_y_in, ry_sem.at[0], ry_sem.at[1], dev(x, z, c, 1 - y))
+    y_copy.start()
+    forward_res(1)
+    y_copy.wait_recv()
+    sums = jnp.sum(red_y[...] + red_y_in[...], axis=1, keepdims=True)
+    gg, gu, uu, qq, qw, ww = [sums[i:i + 1, :] for i in range(6)]
+    step0 = gg / qq
+    next_norm = gg - 2.0 * step0 * gu + step0 * step0 * uu
+    grown = 1.0 + next_norm / gg
+    image_norm = grown * grown * qq - 2.0 * grown * step0 * qw + step0 * step0 * ww
+    step1 = next_norm / image_norm
+    first = step0 + step1 * grown
+    second = -(step1 * step0)
+
+    for l in range(4):
+        for v in range(2):
+            @pl.when(jnp.logical_not(jnp.logical_and(z == l, c == x)))
+            def _():
+                rcopy(grad_half.at[v, 0], sol_in.at[v, l], so_ssem.at[v, 0], so_rsem.at[v, l],
+                      other_core).wait_recv()
+        sol_ref[l] = first * sol_in[0, l].astype(F32) + second * sol_in[1, l].astype(F32)
+    for l in range(4):
+        @pl.when(c != x)
+        def _():
+            for v in range(2):
+                fw_copy(v, l).wait_recv()
+        res_ref[l] = p_ref[l] - (first * res_in[0, l].astype(F32) + second * res_in[1, l].astype(F32))
+
+    gp_copy.wait_send()
+
+    @pl.when(c == half)
+    def _():
+        for shift in range(1, 4):
+            mic_copy(shift).wait_send()
+
+    @pl.when(c == x)
+    def _():
+        wn_copy.wait_send()
+        for shift in range(1, 4):
+            p_copy(shift).wait_send()
+
+        @pl.when(c != half)
+        def _():
+            p_copy(0).wait_send()
+        for v in range(2):
+            for l in range(4):
+                fw_copy(v, l).wait_send()
+    for v in range(2):
+        for k in range(2 * n_grid // BLOCK):
+            ex_copy(v, k).wait_send()
+        for shift in range(1, 4):
+            sol_copy(v, shift).wait_send()
+
+        @pl.when(c != x)
+        def _():
+            sol_copy(v, 0).wait_send()
+        for j in range(2):
+            @pl.when(jnp.logical_not(own_quarter(j)))
+            def _():
+                res_copy(v, j).wait_send()
+    for i in range(len(offsets)):
+        rd_copy(i).wait_send()
+    y_copy.wait_send()
+
+
+def per_chip(grid_points, mic_coords, wavenumbers, pressures):
+    bins, parts, snaps, mics = pressures.shape
+    rows = parts * snaps
+    points = grid_points.shape[1]
+    norm_scale = 1.0 / math.sqrt(points * lax.axis_size("grid"))
+    vmem = pl.BlockSpec(memory_space=pltpu.VMEM)
+    dma = pltpu.SemaphoreType.DMA
+    blocks = 2 * points // BLOCK
+    solution, residual = pl.pallas_call(
+        functools.partial(kernel, norm_scale),
+        out_shape=(jax.ShapeDtypeStruct((bins, rows, points), F32), jax.ShapeDtypeStruct((bins, rows, mics), F32)),
+        in_specs=[vmem, vmem, pl.BlockSpec(memory_space=pltpu.SMEM), vmem],
+        out_specs=(vmem, vmem),
+        scratch_shapes=[
+            pltpu.VMEM((2, 3, points), F32),
+            pltpu.VMEM((2, 3, mics), F32),
+            pltpu.VMEM((8, 128), F32),
+            pltpu.VMEM((3, 2 * points, 128), F32),
+            pltpu.VMEM((2 * points, 2 * mics), BF16),
+            pltpu.VMEM((2 * points, 2 * mics), BF16),
+            pltpu.VMEM((bins, rows, mics), BF16),
+            pltpu.VMEM((2, rows, mics), BF16),
+            pltpu.VMEM((rows, 2 * mics), BF16),
+            pltpu.VMEM((rows, 2 * mics), BF16),
+            pltpu.VMEM((2, rows, 2 * points), F32),
+            pltpu.VMEM((2, rows, 2 * points), F32),
+            pltpu.VMEM((2, rows, 2 * points), F32),
+            pltpu.VMEM((2, rows, 2 * mics), F32),
+            pltpu.VMEM((2, 2, rows, points), BF16),
+            pltpu.VMEM((2, 2, rows, mics), BF16),
+            pltpu.VMEM((2, bins, rows, points), BF16),
+            pltpu.VMEM((2, bins, rows, mics), BF16),
+            pltpu.VMEM((8, 128), F32),
+            pltpu.VMEM((16, 8, 128), F32),
+            pltpu.VMEM((8, 128), F32),
+            pltpu.VMEM((8, 128), F32),
+            dma((5,)), dma((4,)), dma((4,)), dma((2,)),
+            dma((2, blocks)), dma((2, blocks)), dma((2, 4)), dma((2, 4)),
+            dma((2, 2)), dma((2, 4)), dma((2, 4)), dma((15,)), dma((15,)), dma((2,)),
+        ],
+        compiler_params=pltpu.CompilerParams(
+            collective_id=0, has_side_effects=True, vmem_limit_bytes=48 * 1024 * 1024),
+    )(grid_points, mic_coords, wavenumbers, pressures.reshape(bins, rows, mics))
+    return (solution.reshape(bins, parts, snaps, points), residual.reshape(pressures.shape))
+
 
 ITERS = 2
 
@@ -78,8 +466,9 @@
 
 def solution(mesh):
     placed = (P(None, "grid"), P(None, "mic"), P("bin"), P("bin", None, None, "mic"))
+    sizes = (mesh.shape["grid"], mesh.shape["mic"], mesh.shape["bin"])
     return jax.shard_map(
-        body,
+        per_chip if sizes == (2, 4, 4) else body,
         mesh=mesh,
         in_specs=placed,
         out_specs=(P("bin", None, None, "grid"), P("bin", None, None, "mic")),

time: 371 us -> 68.5 us (0.18)
  waiting for transfers between devices: 132 us -> 0 us
  blocking collectives: 93 us -> 0 us
  other arithmetic: 85.2 us -> 0 us
  Pallas kernels: 0 us -> 62.2 us
  matrix products: 33.6 us -> 0 us
  between operations: 17.9 us -> 0.65 us
  local copies, waits for them, and re-layouts: 8.72 us -> 4.71 us
    psum x4 -> x0, waiting for transfers between devices: 131 us -> none  [the longest x2 75.8 us: apply_adjoint(): summed = lax.psum(partial_terms, 'mic')]
    psum x4 -> x0, blocking collectives: 93 us -> none  [the longest x2 66.1 us: body(): image_norm = lax.psum(jnp.sum(apply_summed * apply_summed), ('mic', 'bin'))]
    convert_element_type x4 -> x0, other arithmetic: 70.7 us -> none  [the longest x1 67.4 us: steering_tiles(): cos_list.append((jnp.cos(phase_angle) * amplitude).astype(jnp.bfloat16))]
    pallas_call x0 -> x1, Pallas kernels: none -> 62.2 us  [per_chip(): pl.pallas_call(functools.partial(kernel, norm_scale), out_shape=(jax.Shap...]
    dot_general x8 -> x0, matrix products: 33.6 us -> none  [the longest x2 10 us: body(): jnp.einsum('fkg,fgm->fkm', apply_rounded, cos_tiles, preferred_element_ty...]
    reduce_sum x4 -> x0, other arithmetic: 7.28 us -> none  [the longest x2 3.72 us: apply_adjoint(): grad_norm = lax.psum(jnp.sum(summed * summed), ('grid', 'bin'))]
    another operation x9 -> x0, other arithmetic: 6.02 us -> none  [the longest x1 2.39 us: steering_tiles(): return (jnp.stack(cos_list), jnp.stack(sin_list))]
  transfers between devices with their start and end apart: 4 -> 0, of which waited for: 4 -> 0; matrix products, arithmetic and copies ran while one was open for 0% -> 0% of each run, Pallas kernels for 0% -> 0%
where the time goes in v1:
time: 68.5 us; the launch traced here: 67.6 us
  Pallas kernels  62.2 us (91%)
  local copies, waits for them, and re-layouts  4.71 us (7%)
    pallas_call x1, Pallas kernels, per_chip(): pl.pallas_call(functools.partial(kernel, norm_scale), out_shape=(jax.Shap...  62.2 us
    unnamed x10, local copies, waits for them, and re-layouts  4.71 us

profile of v1, /device:TPU:0, one launch (start us, length us, event | category | flops | bytes accessed | tf_op | source)
XLA Modules:
  0.0 67.6 jit_solution(15820246125411634443)
XLA Ops:
  0.6 0.0 copy-start.3
  0.6 0.6 copy-done.3
  1.3 0.0 copy-start
  1.3 1.0 %copy-done = f32[4,2,16,1024]{3,2,1,0:T(8,128)S(1)} copy-done((f32[4,2,16,1024]{3,2,1,0:T(8,128)S(1)}, f32[4,2,16,1024]{3,2,1,0:T(8,128)}, u32[]{:S(2)}) %copy-start) | copy-done | bytes 524312
  2.3 0.0 copy-start.1
  2.3 0.7 %copy-done.1 = f32[3,1024]{1,0:T(4,128)S(1)} copy-done((f32[3,1024]{1,0:T(4,128)S(1)}, f32[3,1024]{1,0:T(4,128)}, u32[]{:S(2)}) %copy-start.1) | copy-done | bytes 12312
  3.0 0.0 copy-start.2
  3.0 0.7 %copy-done.2 = f32[3,1024]{1,0:T(4,128)S(1)} copy-done((f32[3,1024]{1,0:T(4,128)S(1)}, f32[3,1024]{1,0:T(4,128)}, u32[]{:S(2)}) %copy-start.2) | copy-done | bytes 12312
  3.8 62.2 %shard_map.59 = (f32[4,32,1024]{2,1,0:T(8,128)S(1)}, f32[4,32,1024]{2,1,0:T(8,128)S(1)}) custom-call(f32[3,1024]{1,0:T(4,128)S(1)} %copy-done.1, f32[3,1024]{1,0:T(4,128)S(1)} %copy-done.2, f32[4]{0:T(128)S(1)} %copy-done.3, f32[4,32,1024]{2,1,0:T(8,128)S(1)} %bitcast.3), custom_call_target="tpu_custom_call" | custom-call | tf_op jit(solution)/shard_map/pallas_call | solution.py:358
  66.0 0.8 %copy.8 = f32[4,2,16,1024]{3,2,1,0:T(8,128)} copy(f32[4,2,16,1024]{3,2,1,0:T(8,128)S(1)} %bitcast.5) | data formatting | bytes 1048576
  66.8 0.8 %copy.9 = f32[4,2,16,1024]{3,2,1,0:T(8,128)} copy(f32[4,2,16,1024]{3,2,1,0:T(8,128)S(1)} %bitcast.4) | data formatting | bytes 1048576
Async XLA Ops:
  0.6 0.7 copy-start.3
  1.3 1.0 %copy-start = (f32[4,2,16,1024]{3,2,1,0:T(8,128)S(1)}, f32[4,2,16,1024]{3,2,1,0:T(8,128)}, u32[]{:S(2)}) copy-start(f32[4,2,16,1024]{3,2,1,0:T(8,128)} %param.7) | copy-start | bytes 1572868
  2.3 0.7 %copy-start.1 = (f32[3,1024]{1,0:T(4,128)S(1)}, f32[3,1024]{1,0:T(4,128)}, u32[]{:S(2)}) copy-start(f32[3,1024]{1,0:T(4,128)} %gp_ref.1) | copy-start | bytes 36868
  3.0 0.7 %copy-start.2 = (f32[3,1024]{1,0:T(4,128)S(1)}, f32[3,1024]{1,0:T(4,128)}, u32[]{:S(2)}) copy-start(f32[3,1024]{1,0:T(4,128)} %mc_ref.1) | copy-start | bytes 36868

commit v2 on v1

--- a/solution.py
+++ b/solution.py
@@ -15,7 +15,8 @@
 SIN_COEF = (4.4428679, -7.30744342, 3.59478804, -0.78437393)
 COS_COEF = (1.41420408, -6.97764205, 5.71523831, -1.72834838)
 ROUNDER = 12582912.0
-ROWS = 32
+ROWS = 64
+TILE = 256
 BLOCK = 512
 
 
@@ -27,11 +28,11 @@
 
 
 def kernel(norm_scale, gp_ref, mc_ref, wn_ref, p_ref, sol_ref, res_ref,
-           gp_all, mc_all, wn_buf, gcol, cos_t, sin_t, p_send, p_all, op_a, op_b,
+           gp_all, mc_all, wn_buf, p_loc, g_rows, m_rows, g_mat, m_mat, cos_t, sin_t, p_send, p_all, op_a, op_b,
            part, part_in, grad, image, grad_half, image_half, sol_in, res_in,
            red_out, red_in, red_y, red_y_in,
            co_send, co_recv, p_ssem, p_rsem, ex_ssem, ex_rsem, so_ssem, so_rsem,
-           re_ssem, re_rsem, fw_ssem, rd_ssem, rd_rsem, ry_sem):
+           re_ssem, re_rsem, fw_ssem, rd_ssem, rd_rsem, ry_sem, in_sem):
     x, z, b = lax.axis_index("grid"), lax.axis_index("mic"), lax.axis_index("bin")
     y, c = b // 2, b % 2
     half = z // 2
@@ -57,6 +58,24 @@
     for o in offsets:
         pl.semaphore_signal(barrier, inc=1, device_id=at_offset(o), device_id_type=MESH)
     pl.semaphore_signal(barrier, inc=1, device_id=dev(x, z, c, 1 - y), device_id_type=MESH)
+    p_load = pltpu.make_async_copy(p_ref, p_loc, in_sem.at[0])
+    p_load.start()
+    gp_load = pltpu.make_async_copy(gp_ref, gp_all.at[x], in_sem.at[1])
+    gp_load.start()
+    mc_load = pltpu.make_async_copy(mc_ref, mc_all.at[z % 2], in_sem.at[2])
+    wn_load = pltpu.make_async_copy(wn_ref, wn_buf, in_sem.at[3])
+
+    @pl.when(c == half)
+    def _():
+        mc_load.start()
+
+    @pl.when(c == x)
+    def _():
+        wn_load.start()
+
+    g_rows[...] = jnp.zeros(g_rows.shape, F32)
+    m_rows[...] = jnp.zeros(m_rows.shape, F32)
+    m_mat[...] = jnp.zeros(m_mat.shape, BF16)
     pl.semaphore_wait(barrier, len(offsets) + 1)
 
     gp_copy = rcopy(gp_ref, gp_all.at[x], co_send.at[0], co_recv.at[0], dev(1 - x, z, c))
@@ -70,24 +89,22 @@
     def _():
         for shift in range(1, 4):
             mic_copy(shift).start()
-        mc_all[z % 2] = mc_ref[...]
-
-    wn_copy = rcopy(wn_buf, wn_buf, co_send.at[0 + 4], co_recv.at[3], other_core)
+
+    wn_copy = rcopy(wn_ref, wn_buf, co_send.at[0 + 4], co_recv.at[3], other_core)
 
     @pl.when(c == x)
     def _():
-        wn_buf[...] = jnp.full(wn_buf.shape, wn_ref[z], F32)
         wn_copy.start()
-
-    gp_all[x] = gp_ref[...]
 
     def p_copy(shift):
         to = (z + shift) % 4
         return rcopy(p_send.at[to], p_all.at[z % 2], p_ssem.at[shift], p_rsem.at[z % 2], dev(x, to, half))
 
+    p_load.wait()
+
     @pl.when(c == x)
     def _():
-        p_send[...] = p_ref[...].astype(BF16)
+        p_send[...] = p_loc[...].astype(BF16)
         for shift in range(4):
             if shift:
                 p_copy(shift).start()
@@ -100,6 +117,16 @@
                 def _():
                     p_all[z % 2] = p_send[z]
 
+    gp_load.wait()
+
+    @pl.when(c == half)
+    def _():
+        mc_load.wait()
+
+    @pl.when(c == x)
+    def _():
+        wn_load.wait()
+
     gp_copy.wait_recv()
     for j in range(2):
         @pl.when(z != 2 * c + j)
@@ -110,40 +137,55 @@
     def _():
         wn_copy.wait_recv()
 
-    turns = wn_buf[0:1, 0:1] * (1.0 / (2.0 * math.pi))
-    amp_scale = turns * norm_scale
-    gp_all[...] = gp_all[...] * turns[None]
-    mc_all[...] = mc_all[...] * turns[None]
+    here = lax.broadcasted_iota(jnp.int32, wn_buf.shape, 1) == z
+    wavenumber = jnp.sum(jnp.where(here, wn_buf[...], 0.0), axis=1, keepdims=True)
+    turns = wavenumber * (1.0 / (2.0 * math.pi))
+    scale_row = jnp.broadcast_to(turns * norm_scale, (32, 128))
+
+    def pieces(v):
+        high = v.astype(BF16).astype(F32)
+        rest = v - high
+        mid = rest.astype(BF16).astype(F32)
+        return high, mid, (rest - mid).astype(BF16).astype(F32)
+
+    def fill(out, h, width, left, norm_at, one_at, v):
+        cols = slice(h * width, (h + 1) * width)
+        split = pieces(v)
+        for i, which in enumerate(left):
+            out[3 * i:3 * i + 3, cols] = split[which]
+        for i, value in enumerate(pieces(jnp.sum(v * v, axis=0, keepdims=True))):
+            out[norm_at + i:norm_at + i + 1, cols] = value
+        out[one_at:one_at + 3, cols] = jnp.ones((3, width), F32)
+
     for h in range(2):
-        for d in range(3):
-            for k in range(n_grid // 128):
-                row = gp_all[h, d:d + 1, k * 128:(k + 1) * 128]
-                gcol[d, h * n_grid + k * 128:h * n_grid + (k + 1) * 128, :] = jnp.broadcast_to(row, (128, 128)).T
-
-    scale_row = jnp.broadcast_to(amp_scale, (ROWS, 128))
+        fill(g_rows, h, n_grid, (0, 0, 1, 1, 0, 2), 18, 21, gp_all[h] * turns)
+        fill(m_rows, h, n_mic, (0, 1, 0, 1, 2, 0), 21, 18, mc_all[h] * turns)
+    row_index = lax.broadcasted_iota(jnp.int32, (32, 1), 0)
+    m_mat[0:32, :] = (m_rows[...] * jnp.where(row_index < 18, -2.0, 1.0)).astype(BF16)
+    for k in range(2 * n_grid // 128):
+        g_mat[k * 128:(k + 1) * 128, :] = g_rows[:, k * 128:(k + 1) * 128].T.astype(BF16)
 
     @pl.loop(0, 2 * n_grid // ROWS)
     def _(i):
-        rows = pl.ds(pl.multiple_of(i * ROWS, ROWS), ROWS)
-        gx, gy, gz = gcol[0, rows, :], gcol[1, rows, :], gcol[2, rows, :]
-        for j in range(2):
-            for k in range(n_mic // 128):
-                lanes = slice(k * 128, (k + 1) * 128)
-                dx = gx - mc_all[j, 0:1, lanes]
-                dy = gy - mc_all[j, 1:2, lanes]
-                dz = gz - mc_all[j, 2:3, lanes]
-                q = dx * dx + dy * dy + dz * dz
-                inv = lax.rsqrt(q)
-                t = q * inv
-                amp = inv * scale_row
-                f = t - ((t + ROUNDER) - ROUNDER)
-                s = f * f
-                sine = f * poly(SIN_COEF, s)
-                cosine = poly(COS_COEF, s)
-                scaled = sine * amp
-                cols = slice(j * n_mic + k * 128, j * n_mic + (k + 1) * 128)
-                cos_t[rows, cols] = (amp - scaled * sine).astype(BF16)
-                sin_t[rows, cols] = (scaled * cosine).astype(BF16)
+        base = pl.multiple_of(i * ROWS, ROWS)
+        points = g_mat[pl.ds(base, ROWS), :]
+        for n in range(2 * n_mic // TILE):
+            squares = jnp.dot(points, m_mat[:, n * TILE:(n + 1) * TILE], preferred_element_type=F32)
+            for r in range(ROWS // 32):
+                for k in range(TILE // 128):
+                    q = squares[r * 32:(r + 1) * 32, k * 128:(k + 1) * 128]
+                    inv = lax.rsqrt(q)
+                    t = q * inv
+                    amp = inv * scale_row
+                    f = t - ((t + ROUNDER) - ROUNDER)
+                    s = f * f
+                    sine = f * poly(SIN_COEF, s)
+                    cosine = poly(COS_COEF, s)
+                    scaled = sine * amp
+                    rows = pl.ds(base + r * 32, 32)
+                    cols = slice(n * TILE + k * 128, n * TILE + (k + 1) * 128)
+                    cos_t[rows, cols] = (amp - scaled * sine).astype(BF16)
+                    sin_t[rows, cols] = (scaled * cosine).astype(BF16)
 
     for j in range(2):
         @pl.when(jnp.logical_not(jnp.logical_and(z == 2 * c + j, c == x)))
@@ -308,7 +350,7 @@
         def _():
             for v in range(2):
                 fw_copy(v, l).wait_recv()
-        res_ref[l] = p_ref[l] - (first * res_in[0, l].astype(F32) + second * res_in[1, l].astype(F32))
+        res_ref[l] = p_loc[l] - (first * res_in[0, l].astype(F32) + second * res_in[1, l].astype(F32))
 
     gp_copy.wait_send()
 
@@ -358,13 +400,17 @@
     solution, residual = pl.pallas_call(
         functools.partial(kernel, norm_scale),
         out_shape=(jax.ShapeDtypeStruct((bins, rows, points), F32), jax.ShapeDtypeStruct((bins, rows, mics), F32)),
-        in_specs=[vmem, vmem, pl.BlockSpec(memory_space=pltpu.SMEM), vmem],
+        in_specs=[pl.BlockSpec(memory_space=pltpu.HBM)] * 4,
         out_specs=(vmem, vmem),
         scratch_shapes=[
             pltpu.VMEM((2, 3, points), F32),
             pltpu.VMEM((2, 3, mics), F32),
-            pltpu.VMEM((8, 128), F32),
-            pltpu.VMEM((3, 2 * points, 128), F32),
+            pltpu.VMEM((1, bins), F32),
+            pltpu.VMEM((bins, rows, mics), F32),
+            pltpu.VMEM((128, 2 * points), F32),
+            pltpu.VMEM((32, 2 * mics), F32),
+            pltpu.VMEM((2 * points, 128), BF16),
+            pltpu.VMEM((128, 2 * mics), BF16),
             pltpu.VMEM((2 * points, 2 * mics), BF16),
             pltpu.VMEM((2 * points, 2 * mics), BF16),
             pltpu.VMEM((bins, rows, mics), BF16),
@@ -385,11 +431,11 @@
             pltpu.VMEM((8, 128), F32),
             dma((5,)), dma((4,)), dma((4,)), dma((2,)),
             dma((2, blocks)), dma((2, blocks)), dma((2, 4)), dma((2, 4)),
-            dma((2, 2)), dma((2, 4)), dma((2, 4)), dma((15,)), dma((15,)), dma((2,)),
+            dma((2, 2)), dma((2, 4)), dma((2, 4)), dma((15,)), dma((15,)), dma((2,)), dma((4,)),
         ],
         compiler_params=pltpu.CompilerParams(
             collective_id=0, has_side_effects=True, vmem_limit_bytes=48 * 1024 * 1024),
-    )(grid_points, mic_coords, wavenumbers, pressures.reshape(bins, rows, mics))
+    )(grid_points, mic_coords, wavenumbers.reshape(1, bins), pressures.reshape(bins, rows, mics))
     return (solution.reshape(bins, parts, snaps, points), residual.reshape(pressures.shape))
 
 

time: 68.5 us -> 67.7 us (0.988)
  Pallas kernels: 62.2 us -> 61.5 us
    pallas_call x1, Pallas kernels: 62.2 us -> 61.5 us  [per_chip(): pl.pallas_call(functools.partial(kernel, norm_scale), out_shape=(jax.Shap...]
where the time goes in v2:
time: 67.7 us; the launch traced here: 66.8 us
  Pallas kernels  61.5 us (91%)
  local copies, waits for them, and re-layouts  4.71 us (7%)
    pallas_call x1, Pallas kernels, per_chip(): pl.pallas_call(functools.partial(kernel, norm_scale), out_shape=(jax.Shap...  61.5 us
    unnamed x10, local copies, waits for them, and re-layouts  4.71 us

profile of v2, /device:TPU:0, one launch (start us, length us, event | category | flops | bytes accessed | tf_op | source)
XLA Modules:
  0.0 66.8 jit_solution(4953768436869704141)
XLA Ops:
  0.6 0.0 copy-start.3
  0.6 0.6 copy-done.3
  1.3 0.0 copy-start
  1.3 1.0 %copy-done = f32[4,2,16,1024]{3,2,1,0:T(8,128)S(1)} copy-done((f32[4,2,16,1024]{3,2,1,0:T(8,128)S(1)}, f32[4,2,16,1024]{3,2,1,0:T(8,128)}, u32[]{:S(2)}) %copy-start) | copy-done | bytes 524312
  2.3 0.0 copy-start.1
  2.3 0.7 %copy-done.1 = f32[3,1024]{1,0:T(4,128)S(1)} copy-done((f32[3,1024]{1,0:T(4,128)S(1)}, f32[3,1024]{1,0:T(4,128)}, u32[]{:S(2)}) %copy-start.1) | copy-done | bytes 12312
  3.0 0.0 copy-start.2
  3.0 0.7 %copy-done.2 = f32[3,1024]{1,0:T(4,128)S(1)} copy-done((f32[3,1024]{1,0:T(4,128)S(1)}, f32[3,1024]{1,0:T(4,128)}, u32[]{:S(2)}) %copy-start.2) | copy-done | bytes 12312
  3.8 61.5 %shard_map.59 = (f32[4,32,1024]{2,1,0:T(8,128)S(1)}, f32[4,32,1024]{2,1,0:T(8,128)S(1)}) custom-call(f32[3,1024]{1,0:T(4,128)S(1)} %copy-done.1, f32[3,1024]{1,0:T(4,128)S(1)} %copy-done.2, f32[1,4]{1,0:T(1,128)S(1)} %bitcast.7, f32[4,32,1024]{2,1,0:T(8,128)S(1)} %bitcast.4), custom_call_target="tpu_custom_call" | custom-call | tf_op jit(solution)/shard_map/pallas_call | solution.py:400
  65.2 0.8 %copy.8 = f32[4,2,16,1024]{3,2,1,0:T(8,128)} copy(f32[4,2,16,1024]{3,2,1,0:T(8,128)S(1)} %bitcast.6) | data formatting | bytes 1048576
  66.0 0.8 %copy.9 = f32[4,2,16,1024]{3,2,1,0:T(8,128)} copy(f32[4,2,16,1024]{3,2,1,0:T(8,128)S(1)} %bitcast.5) | data formatting | bytes 1048576
Async XLA Ops:
  0.6 0.7 copy-start.3
  1.3 1.0 %copy-start = (f32[4,2,16,1024]{3,2,1,0:T(8,128)S(1)}, f32[4,2,16,1024]{3,2,1,0:T(8,128)}, u32[]{:S(2)}) copy-start(f32[4,2,16,1024]{3,2,1,0:T(8,128)} %param.7) | copy-start | bytes 1572868
  2.3 0.7 %copy-start.1 = (f32[3,1024]{1,0:T(4,128)S(1)}, f32[3,1024]{1,0:T(4,128)}, u32[]{:S(2)}) copy-start(f32[3,1024]{1,0:T(4,128)} %gp_ref.1) | copy-start | bytes 36868
  3.0 0.7 %copy-start.2 = (f32[3,1024]{1,0:T(4,128)S(1)}, f32[3,1024]{1,0:T(4,128)}, u32[]{:S(2)}) copy-start(f32[3,1024]{1,0:T(4,128)} %mc_ref.1) | copy-start | bytes 36868

commit v3 on v2

--- a/solution.py
+++ b/solution.py
@@ -28,11 +28,11 @@
 
 
 def kernel(norm_scale, gp_ref, mc_ref, wn_ref, p_ref, sol_ref, res_ref,
-           gp_all, mc_all, wn_buf, p_loc, g_rows, m_rows, g_mat, m_mat, cos_t, sin_t, p_send, p_all, op_a, op_b,
+           gp_all, mc_all, wn_buf, p_loc, g_rows, m_rows, g_mat, m_mat, sq_even, sq_odd, cos_t, sin_t, p_send, p_all, op_a, op_b, col_a, col_b,
            part, part_in, grad, image, grad_half, image_half, sol_in, res_in,
            red_out, red_in, red_y, red_y_in,
            co_send, co_recv, p_ssem, p_rsem, ex_ssem, ex_rsem, so_ssem, so_rsem,
-           re_ssem, re_rsem, fw_ssem, rd_ssem, rd_rsem, ry_sem, in_sem):
+           re_ssem, re_rsem, fw_ssem, rd_ssem, rd_rsem, ry_sem, in_sem, rl_ssem):
     x, z, b = lax.axis_index("grid"), lax.axis_index("mic"), lax.axis_index("bin")
     y, c = b // 2, b % 2
     half = z // 2
@@ -165,41 +165,59 @@
     for k in range(2 * n_grid // 128):
         g_mat[k * 128:(k + 1) * 128, :] = g_rows[:, k * 128:(k + 1) * 128].T.astype(BF16)
 
-    @pl.loop(0, 2 * n_grid // ROWS)
+    def squares(i, out):
+        points = g_mat[pl.ds(pl.multiple_of(i * ROWS, ROWS), ROWS), :]
+        for n in range(2 * n_mic // TILE):
+            cols = slice(n * TILE, (n + 1) * TILE)
+            out[:, cols] = jnp.dot(points, m_mat[:, cols], preferred_element_type=F32)
+
+    def tiles(i, source):
+        base = pl.multiple_of(i * ROWS, ROWS)
+        for k in range(2 * n_mic // 128):
+            cols = slice(k * 128, (k + 1) * 128)
+            for r in range(0, ROWS, 32):
+                q = source[r:r + 32, cols]
+                inv = lax.rsqrt(q)
+                t = q * inv
+                amp = inv * scale_row
+                f = t - ((t + ROUNDER) - ROUNDER)
+                s = f * f
+                sine = f * poly(SIN_COEF, s)
+                cosine = poly(COS_COEF, s)
+                scaled = sine * amp
+                rows = pl.ds(base + r, 32)
+                cos_t[rows, cols] = (amp - scaled * sine).astype(BF16)
+                sin_t[rows, cols] = (scaled * cosine).astype(BF16)
+
+    steps = 2 * n_grid // ROWS
+    squares(0, sq_even)
+
+    @pl.loop(0, steps // 2)
     def _(i):
-        base = pl.multiple_of(i * ROWS, ROWS)
-        points = g_mat[pl.ds(base, ROWS), :]
-        for n in range(2 * n_mic // TILE):
-            squares = jnp.dot(points, m_mat[:, n * TILE:(n + 1) * TILE], preferred_element_type=F32)
-            for r in range(ROWS // 32):
-                for k in range(TILE // 128):
-                    q = squares[r * 32:(r + 1) * 32, k * 128:(k + 1) * 128]
-                    inv = lax.rsqrt(q)
-                    t = q * inv
-                    amp = inv * scale_row
-                    f = t - ((t + ROUNDER) - ROUNDER)
-                    s = f * f
-                    sine = f * poly(SIN_COEF, s)
-                    cosine = poly(COS_COEF, s)
-                    scaled = sine * amp
-                    rows = pl.ds(base + r * 32, 32)
-                    cols = slice(n * TILE + k * 128, n * TILE + (k + 1) * 128)
-                    cos_t[rows, cols] = (amp - scaled * sine).astype(BF16)
-                    sin_t[rows, cols] = (scaled * cosine).astype(BF16)
+        squares(2 * i + 1, sq_odd)
+        tiles(2 * i, sq_even)
+        squares(jnp.minimum(2 * i + 2, steps - 1), sq_even)
+        tiles(2 * i + 1, sq_odd)
 
     for j in range(2):
         @pl.when(jnp.logical_not(jnp.logical_and(z == 2 * c + j, c == x)))
         def _():
             rcopy(p_send.at[0], p_all.at[j], p_ssem.at[0], p_rsem.at[j], other_core).wait_recv()
 
-    def operands(blocks, adjoint):
+    def forward_operands(blocks):
         for j in range(2):
             v = blocks[j]
-            real, imag = v[:16], v[16:]
-            swapped = [-imag, real] if adjoint else [imag, -real]
             cols = slice(j * v.shape[1], (j + 1) * v.shape[1])
             op_a[:, cols] = v
-            op_b[:, cols] = jnp.concatenate(swapped, axis=0)
+            op_b[:, cols] = jnp.concatenate([v[16:], -v[:16]], axis=0)
+
+    def adjoint_operands(blocks):
+        for j in range(2):
+            for k in range(n_mic // 128):
+                v = blocks[j, :, k * 128:(k + 1) * 128].astype(F32)
+                rows = slice(j * n_mic + k * 128, j * n_mic + (k + 1) * 128)
+                col_a[rows, :] = v.T.astype(BF16)
+                col_b[rows, :] = jnp.concatenate([-v[16:], v[:16]], axis=0).T.astype(BF16)
 
     def products(accs, pairs):
         out = []
@@ -215,10 +233,11 @@
     def adjoint(v):
         for k in range(2 * n_grid // BLOCK):
             rows = slice(k * BLOCK, (k + 1) * BLOCK)
-            dims = (((1,), (1,)), ((), ()))
-            part[v, :, rows] = (
-                lax.dot_general(op_a[...], cos_t[rows, :], dims, preferred_element_type=F32)
-                + lax.dot_general(op_b[...], sin_t[rows, :], dims, preferred_element_type=F32))
+            columns = (jnp.dot(cos_t[rows, :], col_a[...], preferred_element_type=F32)
+                       + jnp.dot(sin_t[rows, :], col_b[...], preferred_element_type=F32))
+            for m in range(BLOCK // 128):
+                low = k * BLOCK + m * 128
+                part[v, :, low:low + 128] = columns[m * 128:(m + 1) * 128].T
             ex_copy(v, k).start()
         for k in range(2 * n_grid // BLOCK):
             cols = slice(k * BLOCK, (k + 1) * BLOCK)
@@ -238,20 +257,35 @@
             image_half[v, h, :, low:low + BLOCK] = total.astype(BF16)
 
     def sol_copy(v, shift):
-        to = (z + shift) % 4
+        to = z // 2 + shift
         return rcopy(grad_half.at[v, c], sol_in.at[v, z], so_ssem.at[v, shift], so_rsem.at[v, z], dev(c, to, x))
 
+    def own_block(shift):
+        return jnp.logical_and(z // 2 + shift == z, c == x)
+
     def send_sol(v):
-        for shift in range(1, 4):
-            sol_copy(v, shift).start()
-
-        @pl.when(c != x)
-        def _():
-            sol_copy(v, 0).start()
+        for shift in range(3):
+            @pl.when(jnp.logical_not(own_block(shift)))
+            def _():
+                sol_copy(v, shift).start()
 
         @pl.when(c == x)
         def _():
             sol_in[v, z] = grad_half[v, c]
+
+    relays = jnp.logical_or(z == 1, z == 2)
+
+    def relay_copy(v, i):
+        l = jnp.where(z == 2, i, 2 + i)
+        return rcopy(sol_in.at[v, l], sol_in.at[v, l], rl_ssem.at[v, i], so_rsem.at[v, l],
+                     dev(x, jnp.where(z == 2, 3, 0), c))
+
+    def relay_sol(v):
+        @pl.when(relays)
+        def _():
+            for i in range(2):
+                relay_copy(v, i).wait_recv()
+                relay_copy(v, i).start()
 
     def res_copy(v, j):
         return rcopy(image_half.at[v, j], res_in.at[v, z], re_ssem.at[v, j], re_rsem.at[v, z], dev(x, 2 * c + j, x))
@@ -281,19 +315,21 @@
                     fw_copy(v, l).wait_recv()
                 fw_copy(v, l).start()
 
-    operands([p_all[0], p_all[1]], True)
+    adjoint_operands(p_all)
     adjoint(0)
     send_sol(0)
-    operands([grad_half[0, 0], grad_half[0, 1]], False)
+    forward_operands([grad_half[0, 0], grad_half[0, 1]])
     forward(0)
     send_res(0)
-    operands([image_half[0, 0], image_half[0, 1]], True)
+    adjoint_operands(image_half.at[0])
     adjoint(1)
     send_sol(1)
-    operands([grad_half[1, 0], grad_half[1, 1]], False)
+    relay_sol(0)
+    forward_operands([grad_half[1, 0], grad_half[1, 1]])
     forward(1)
     send_res(1)
     forward_res(0)
+    relay_sol(1)
 
     zero = jnp.zeros((8, 128), F32)
     accs = [zero] * 6
@@ -340,7 +376,9 @@
 
     for l in range(4):
         for v in range(2):
-            @pl.when(jnp.logical_not(jnp.logical_and(z == l, c == x)))
+            relayed = jnp.logical_and(relays, (z == 2) if l < 2 else (z == 1))
+
+            @pl.when(jnp.logical_not(jnp.logical_or(relayed, jnp.logical_and(z == l, c == x))))
             def _():
                 rcopy(grad_half.at[v, 0], sol_in.at[v, l], so_ssem.at[v, 0], so_rsem.at[v, l],
                       other_core).wait_recv()
@@ -374,12 +412,15 @@
     for v in range(2):
         for k in range(2 * n_grid // BLOCK):
             ex_copy(v, k).wait_send()
-        for shift in range(1, 4):
-            sol_copy(v, shift).wait_send()
-
-        @pl.when(c != x)
-        def _():
-            sol_copy(v, 0).wait_send()
+        for shift in range(3):
+            @pl.when(jnp.logical_not(own_block(shift)))
+            def _():
+                sol_copy(v, shift).wait_send()
+
+        @pl.when(relays)
+        def _():
+            for i in range(2):
+                relay_copy(v, i).wait_send()
         for j in range(2):
             @pl.when(jnp.logical_not(own_quarter(j)))
             def _():
@@ -411,12 +452,16 @@
             pltpu.VMEM((32, 2 * mics), F32),
             pltpu.VMEM((2 * points, 128), BF16),
             pltpu.VMEM((128, 2 * mics), BF16),
+            pltpu.VMEM((ROWS, 2 * mics), F32),
+            pltpu.VMEM((ROWS, 2 * mics), F32),
             pltpu.VMEM((2 * points, 2 * mics), BF16),
             pltpu.VMEM((2 * points, 2 * mics), BF16),
             pltpu.VMEM((bins, rows, mics), BF16),
             pltpu.VMEM((2, rows, mics), BF16),
             pltpu.VMEM((rows, 2 * mics), BF16),
             pltpu.VMEM((rows, 2 * mics), BF16),
+            pltpu.VMEM((2 * mics, rows), BF16),
+            pltpu.VMEM((2 * mics, rows), BF16),
             pltpu.VMEM((2, rows, 2 * points), F32),
             pltpu.VMEM((2, rows, 2 * points), F32),
             pltpu.VMEM((2, rows, 2 * points), F32),
@@ -431,7 +476,7 @@
             pltpu.VMEM((8, 128), F32),
             dma((5,)), dma((4,)), dma((4,)), dma((2,)),
             dma((2, blocks)), dma((2, blocks)), dma((2, 4)), dma((2, 4)),
-            dma((2, 2)), dma((2, 4)), dma((2, 4)), dma((15,)), dma((15,)), dma((2,)), dma((4,)),
+            dma((2, 2)), dma((2, 4)), dma((2, 4)), dma((15,)), dma((15,)), dma((2,)), dma((4,)), dma((2, 2)),
         ],
         compiler_params=pltpu.CompilerParams(
             collective_id=0, has_side_effects=True, vmem_limit_bytes=48 * 1024 * 1024),

time: 67.7 us -> 76.4 us (1.13)
  Pallas kernels: 61.5 us -> 69.8 us
    pallas_call x1, Pallas kernels: 61.5 us -> 69.8 us  [per_chip(): pl.pallas_call(functools.partial(kernel, norm_scale), out_shape=(jax.Shap...]
where the time goes in v3:
time: 76.4 us; the launch traced here: 75.2 us
  Pallas kernels  69.8 us (91%)
  local copies, waits for them, and re-layouts  4.71 us (6%)
    pallas_call x1, Pallas kernels, per_chip(): pl.pallas_call(functools.partial(kernel, norm_scale), out_shape=(jax.Shap...  69.8 us
    unnamed x10, local copies, waits for them, and re-layouts  4.71 us

profile of v3, /device:TPU:0, one launch (start us, length us, event | category | flops | bytes accessed | tf_op | source)
XLA Modules:
  0.0 75.2 jit_solution(3344166814711858538)
XLA Ops:
  0.6 0.0 copy-start.3
  0.6 0.6 copy-done.3
  1.3 0.0 copy-start
  1.3 1.0 %copy-done = f32[4,2,16,1024]{3,2,1,0:T(8,128)S(1)} copy-done((f32[4,2,16,1024]{3,2,1,0:T(8,128)S(1)}, f32[4,2,16,1024]{3,2,1,0:T(8,128)}, u32[]{:S(2)}) %copy-start) | copy-done | bytes 524312
  2.3 0.0 copy-start.1
  2.3 0.7 copy-done.1
  3.0 0.0 copy-start.2
  3.0 0.7 copy-done.2
  3.8 69.8 %shard_map.59 = (f32[4,32,1024]{2,1,0:T(8,128)S(1)}, f32[4,32,1024]{2,1,0:T(8,128)S(1)}) custom-call(f32[3,1024]{1,0:T(4,128)S(1)} %copy-done.1, f32[3,1024]{1,0:T(4,128)S(1)} %copy-done.2, f32[1,4]{1,0:T(1,128)S(1)} %bitcast.7, f32[4,32,1024]{2,1,0:T(8,128)S(1)} %bitcast.4), custom_call_target="tpu_custom_call" | custom-call | tf_op jit(solution)/shard_map/pallas_call | solution.py:441
  73.6 0.8 %copy.8 = f32[4,2,16,1024]{3,2,1,0:T(8,128)} copy(f32[4,2,16,1024]{3,2,1,0:T(8,128)S(1)} %bitcast.6) | data formatting | bytes 1048576
  74.4 0.8 %copy.9 = f32[4,2,16,1024]{3,2,1,0:T(8,128)} copy(f32[4,2,16,1024]{3,2,1,0:T(8,128)S(1)} %bitcast.5) | data formatting | bytes 1048576
Async XLA Ops:
  0.6 0.7 copy-start.3
  1.3 1.0 %copy-start = (f32[4,2,16,1024]{3,2,1,0:T(8,128)S(1)}, f32[4,2,16,1024]{3,2,1,0:T(8,128)}, u32[]{:S(2)}) copy-start(f32[4,2,16,1024]{3,2,1,0:T(8,128)} %param.7) | copy-start | bytes 1572868
  2.3 0.7 copy-start.1
  3.0 0.7 copy-start.2

commit v4 on v2

--- a/solution.py
+++ b/solution.py
@@ -32,7 +32,7 @@
            part, part_in, grad, image, grad_half, image_half, sol_in, res_in,
            red_out, red_in, red_y, red_y_in,
            co_send, co_recv, p_ssem, p_rsem, ex_ssem, ex_rsem, so_ssem, so_rsem,
-           re_ssem, re_rsem, fw_ssem, rd_ssem, rd_rsem, ry_sem, in_sem):
+           re_ssem, re_rsem, fw_ssem, rd_ssem, rd_rsem, ry_sem, in_sem, rl_ssem):
     x, z, b = lax.axis_index("grid"), lax.axis_index("mic"), lax.axis_index("bin")
     y, c = b // 2, b % 2
     half = z // 2
@@ -238,20 +238,35 @@
             image_half[v, h, :, low:low + BLOCK] = total.astype(BF16)
 
     def sol_copy(v, shift):
-        to = (z + shift) % 4
+        to = z // 2 + shift
         return rcopy(grad_half.at[v, c], sol_in.at[v, z], so_ssem.at[v, shift], so_rsem.at[v, z], dev(c, to, x))
 
+    def own_block(shift):
+        return jnp.logical_and(z // 2 + shift == z, c == x)
+
     def send_sol(v):
-        for shift in range(1, 4):
-            sol_copy(v, shift).start()
-
-        @pl.when(c != x)
-        def _():
-            sol_copy(v, 0).start()
+        for shift in range(3):
+            @pl.when(jnp.logical_not(own_block(shift)))
+            def _():
+                sol_copy(v, shift).start()
 
         @pl.when(c == x)
         def _():
             sol_in[v, z] = grad_half[v, c]
+
+    relays = jnp.logical_or(z == 1, z == 2)
+
+    def relay_copy(v, i):
+        l = jnp.where(z == 2, i, 2 + i)
+        return rcopy(sol_in.at[v, l], sol_in.at[v, l], rl_ssem.at[v, i], so_rsem.at[v, l],
+                     dev(x, jnp.where(z == 2, 3, 0), c))
+
+    def relay_sol(v):
+        @pl.when(relays)
+        def _():
+            for i in range(2):
+                relay_copy(v, i).wait_recv()
+                relay_copy(v, i).start()
 
     def res_copy(v, j):
         return rcopy(image_half.at[v, j], res_in.at[v, z], re_ssem.at[v, j], re_rsem.at[v, z], dev(x, 2 * c + j, x))
@@ -290,10 +305,9 @@
     operands([image_half[0, 0], image_half[0, 1]], True)
     adjoint(1)
     send_sol(1)
+    relay_sol(0)
     operands([grad_half[1, 0], grad_half[1, 1]], False)
     forward(1)
-    send_res(1)
-    forward_res(0)
 
     zero = jnp.zeros((8, 128), F32)
     accs = [zero] * 6
@@ -317,6 +331,9 @@
 
     for i in range(len(offsets)):
         rd_copy(i).start()
+    send_res(1)
+    forward_res(0)
+    relay_sol(1)
     red_in[me] = red_out[...]
     for i in range(len(offsets)):
         rd_copy(i).wait_recv()
@@ -340,7 +357,9 @@
 
     for l in range(4):
         for v in range(2):
-            @pl.when(jnp.logical_not(jnp.logical_and(z == l, c == x)))
+            relayed = jnp.logical_and(relays, (z == 2) if l < 2 else (z == 1))
+
+            @pl.when(jnp.logical_not(jnp.logical_or(relayed, jnp.logical_and(z == l, c == x))))
             def _():
                 rcopy(grad_half.at[v, 0], sol_in.at[v, l], so_ssem.at[v, 0], so_rsem.at[v, l],
                       other_core).wait_recv()
@@ -374,12 +393,15 @@
     for v in range(2):
         for k in range(2 * n_grid // BLOCK):
             ex_copy(v, k).wait_send()
-        for shift in range(1, 4):
-            sol_copy(v, shift).wait_send()
-
-        @pl.when(c != x)
-        def _():
-            sol_copy(v, 0).wait_send()
+        for shift in range(3):
+            @pl.when(jnp.logical_not(own_block(shift)))
+            def _():
+                sol_copy(v, shift).wait_send()
+
+        @pl.when(relays)
+        def _():
+            for i in range(2):
+                relay_copy(v, i).wait_send()
         for j in range(2):
             @pl.when(jnp.logical_not(own_quarter(j)))
             def _():
@@ -431,7 +453,7 @@
             pltpu.VMEM((8, 128), F32),
             dma((5,)), dma((4,)), dma((4,)), dma((2,)),
             dma((2, blocks)), dma((2, blocks)), dma((2, 4)), dma((2, 4)),
-            dma((2, 2)), dma((2, 4)), dma((2, 4)), dma((15,)), dma((15,)), dma((2,)), dma((4,)),
+            dma((2, 2)), dma((2, 4)), dma((2, 4)), dma((15,)), dma((15,)), dma((2,)), dma((4,)), dma((2, 2)),
         ],
         compiler_params=pltpu.CompilerParams(
             collective_id=0, has_side_effects=True, vmem_limit_bytes=48 * 1024 * 1024),

time: 67.7 us -> 64.8 us (0.957)
  Pallas kernels: 61.5 us -> 59.1 us
    pallas_call x1, Pallas kernels: 61.5 us -> 59.1 us  [per_chip(): pl.pallas_call(functools.partial(kernel, norm_scale), out_shape=(jax.Shap...]
where the time goes in v4:
time: 64.8 us; the launch traced here: 64.5 us
  Pallas kernels  59.1 us (91%)
  local copies, waits for them, and re-layouts  4.71 us (7%)
  between operations  0.65 us (1%)
    pallas_call x1, Pallas kernels, per_chip(): pl.pallas_call(functools.partial(kernel, norm_scale), out_shape=(jax.Shap...  59.1 us
    unnamed x10, local copies, waits for them, and re-layouts  4.71 us

profile of v4, /device:TPU:0, one launch (start us, length us, event | category | flops | bytes accessed | tf_op | source)
XLA Modules:
  0.0 64.5 jit_solution(7588797612931574321)
XLA Ops:
  0.6 0.0 copy-start.3
  0.6 0.6 %copy-done.3 = f32[4]{0:T(128)S(1)} copy-done((f32[4]{0:T(128)S(1)}, f32[4]{0:T(128)}, u32[]{:S(2)}) %copy-start.3) | copy-done | bytes 40
  1.3 0.0 copy-start
  1.3 1.0 %copy-done = f32[4,2,16,1024]{3,2,1,0:T(8,128)S(1)} copy-done((f32[4,2,16,1024]{3,2,1,0:T(8,128)S(1)}, f32[4,2,16,1024]{3,2,1,0:T(8,128)}, u32[]{:S(2)}) %copy-start) | copy-done | bytes 524312
  2.3 0.0 copy-start.1
  2.3 0.7 %copy-done.1 = f32[3,1024]{1,0:T(4,128)S(1)} copy-done((f32[3,1024]{1,0:T(4,128)S(1)}, f32[3,1024]{1,0:T(4,128)}, u32[]{:S(2)}) %copy-start.1) | copy-done | bytes 12312
  3.0 0.0 copy-start.2
  3.0 0.7 %copy-done.2 = f32[3,1024]{1,0:T(4,128)S(1)} copy-done((f32[3,1024]{1,0:T(4,128)S(1)}, f32[3,1024]{1,0:T(4,128)}, u32[]{:S(2)}) %copy-start.2) | copy-done | bytes 12312
  3.8 59.1 %shard_map.59 = (f32[4,32,1024]{2,1,0:T(8,128)S(1)}, f32[4,32,1024]{2,1,0:T(8,128)S(1)}) custom-call(f32[3,1024]{1,0:T(4,128)S(1)} %copy-done.1, f32[3,1024]{1,0:T(4,128)S(1)} %copy-done.2, f32[1,4]{1,0:T(1,128)S(1)} %bitcast.7, f32[4,32,1024]{2,1,0:T(8,128)S(1)} %bitcast.4), custom_call_target="tpu_custom_call" | custom-call | tf_op jit(solution)/shard_map/pallas_call | solution.py:422
  62.9 0.8 %copy.8 = f32[4,2,16,1024]{3,2,1,0:T(8,128)} copy(f32[4,2,16,1024]{3,2,1,0:T(8,128)S(1)} %bitcast.6) | data formatting | bytes 1048576
  63.7 0.8 %copy.9 = f32[4,2,16,1024]{3,2,1,0:T(8,128)} copy(f32[4,2,16,1024]{3,2,1,0:T(8,128)S(1)} %bitcast.5) | data formatting | bytes 1048576
Async XLA Ops:
  0.6 0.7 %copy-start.3 = (f32[4]{0:T(128)S(1)}, f32[4]{0:T(128)}, u32[]{:S(2)}) copy-start(f32[4]{0:T(128)} %param.6) | copy-start | bytes 52
  1.3 1.0 %copy-start = (f32[4,2,16,1024]{3,2,1,0:T(8,128)S(1)}, f32[4,2,16,1024]{3,2,1,0:T(8,128)}, u32[]{:S(2)}) copy-start(f32[4,2,16,1024]{3,2,1,0:T(8,128)} %param.7) | copy-start | bytes 1572868
  2.3 0.7 %copy-start.1 = (f32[3,1024]{1,0:T(4,128)S(1)}, f32[3,1024]{1,0:T(4,128)}, u32[]{:S(2)}) copy-start(f32[3,1024]{1,0:T(4,128)} %gp_ref.1) | copy-start | bytes 36868
  3.0 0.7 %copy-start.2 = (f32[3,1024]{1,0:T(4,128)S(1)}, f32[3,1024]{1,0:T(4,128)}, u32[]{:S(2)}) copy-start(f32[3,1024]{1,0:T(4,128)} %mc_ref.1) | copy-start | bytes 36868

commit v5 on v4

--- a/solution.py
+++ b/solution.py
@@ -15,7 +15,7 @@
 SIN_COEF = (4.4428679, -7.30744342, 3.59478804, -0.78437393)
 COS_COEF = (1.41420408, -6.97764205, 5.71523831, -1.72834838)
 ROUNDER = 12582912.0
-ROWS = 64
+ROWS = 128
 TILE = 256
 BLOCK = 512
 
@@ -456,7 +456,7 @@
             dma((2, 2)), dma((2, 4)), dma((2, 4)), dma((15,)), dma((15,)), dma((2,)), dma((4,)), dma((2, 2)),
         ],
         compiler_params=pltpu.CompilerParams(
-            collective_id=0, has_side_effects=True, vmem_limit_bytes=48 * 1024 * 1024),
+            collective_id=0, has_side_effects=True, vmem_limit_bytes=64 * 1024 * 1024 - 65536),
     )(grid_points, mic_coords, wavenumbers.reshape(1, bins), pressures.reshape(bins, rows, mics))
     return (solution.reshape(bins, parts, snaps, points), residual.reshape(pressures.shape))
 

time: 64.8 us -> 61.9 us (0.955)
  local copies, waits for them, and re-layouts: 4.71 us -> 2.74 us
  Pallas kernels: 59.1 us -> 58.4 us
    unnamed x10 -> x4, local copies, waits for them, and re-layouts: 4.71 us -> 2.74 us
    pallas_call x1, Pallas kernels: 59.1 us -> 58.4 us  [per_chip(): pl.pallas_call(functools.partial(kernel, norm_scale), out_shape=(jax.Shap...]
where the time goes in v5:
time: 61.9 us; the launch traced here: 61.8 us
  Pallas kernels  58.4 us (94%)
  local copies, waits for them, and re-layouts  2.74 us (4%)
  between operations  0.65 us (1%)
    pallas_call x1, Pallas kernels, per_chip(): pl.pallas_call(functools.partial(kernel, norm_scale), out_shape=(jax.Shap...  58.4 us
    unnamed x4, local copies, waits for them, and re-layouts  2.74 us

profile of v5, /device:TPU:0, one launch (start us, length us, event | category | flops | bytes accessed | tf_op | source)
XLA Modules:
  0.0 61.8 jit_solution(7491043503934136418)
XLA Ops:
  0.6 58.4 %shard_map.59 = (f32[4,32,1024]{2,1,0:T(8,128)}, f32[4,32,1024]{2,1,0:T(8,128)}) custom-call(f32[3,1024]{1,0:T(4,128)} %gp_ref.1, f32[3,1024]{1,0:T(4,128)} %mc_ref.1, f32[1,4]{1,0:T(1,128)} %bitcast.7, f32[4,32,1024]{2,1,0:T(8,128)} %bitcast.4), custom_call_target="tpu_custom_call" | custom-call | tf_op jit(solution)/shard_map/pallas_call | solution.py:422
  59.0 0.0 copy-start
  59.1 1.9 %copy.8 = f32[4,2,16,1024]{3,2,1,0:T(8,128)} copy(f32[4,2,16,1024]{3,2,1,0:T(8,128)} %bitcast.6) | data formatting | bytes 1048576
  61.0 0.0 copy-done
  61.0 0.8 %copy.9 = f32[4,2,16,1024]{3,2,1,0:T(8,128)} copy(f32[4,2,16,1024]{3,2,1,0:T(8,128)S(1)} %bitcast.5) | data formatting | bytes 1048576
Async XLA Ops:
  59.0 2.0 %copy-start = (f32[4,32,1024]{2,1,0:T(8,128)S(1)}, f32[4,32,1024]{2,1,0:T(8,128)}, u32[]{:S(2)}) copy-start(f32[4,32,1024]{2,1,0:T(8,128)} %get-tuple-element.5) | copy-start | bytes 1572868

commit v6 on v5

--- a/solution.py
+++ b/solution.py
@@ -15,7 +15,7 @@
 SIN_COEF = (4.4428679, -7.30744342, 3.59478804, -0.78437393)
 COS_COEF = (1.41420408, -6.97764205, 5.71523831, -1.72834838)
 ROUNDER = 12582912.0
-ROWS = 128
+ROWS = 256
 TILE = 256
 BLOCK = 512
 

time: 61.9 us -> 60.8 us (0.982)
  Pallas kernels: 58.4 us -> 57.3 us
    pallas_call x1, Pallas kernels: 58.4 us -> 57.3 us  [per_chip(): pl.pallas_call(functools.partial(kernel, norm_scale), out_shape=(jax.Shap...]
where the time goes in v6:
time: 60.8 us; the launch traced here: 60.7 us
  Pallas kernels  57.3 us (94%)
  local copies, waits for them, and re-layouts  2.74 us (5%)
  between operations  0.65 us (1%)
    pallas_call x1, Pallas kernels, per_chip(): pl.pallas_call(functools.partial(kernel, norm_scale), out_shape=(jax.Shap...  57.3 us
    unnamed x4, local copies, waits for them, and re-layouts  2.74 us

profile of v6, /device:TPU:0, one launch (start us, length us, event | category | flops | bytes accessed | tf_op | source)
XLA Modules:
  0.0 60.7 jit_solution(14217358565025377406)
XLA Ops:
  0.6 57.3 %shard_map.59 = (f32[4,32,1024]{2,1,0:T(8,128)}, f32[4,32,1024]{2,1,0:T(8,128)}) custom-call(f32[3,1024]{1,0:T(4,128)} %gp_ref.1, f32[3,1024]{1,0:T(4,128)} %mc_ref.1, f32[1,4]{1,0:T(1,128)} %bitcast.7, f32[4,32,1024]{2,1,0:T(8,128)} %bitcast.4), custom_call_target="tpu_custom_call" | custom-call | tf_op jit(solution)/shard_map/pallas_call | solution.py:422
  57.9 0.0 copy-start
  57.9 1.9 %copy.8 = f32[4,2,16,1024]{3,2,1,0:T(8,128)} copy(f32[4,2,16,1024]{3,2,1,0:T(8,128)} %bitcast.6) | data formatting | bytes 1048576
  59.9 0.0 copy-done
  59.9 0.8 %copy.9 = f32[4,2,16,1024]{3,2,1,0:T(8,128)} copy(f32[4,2,16,1024]{3,2,1,0:T(8,128)S(1)} %bitcast.5) | data formatting | bytes 1048576
Async XLA Ops:
  57.9 2.0 %copy-start = (f32[4,32,1024]{2,1,0:T(8,128)S(1)}, f32[4,32,1024]{2,1,0:T(8,128)}, u32[]{:S(2)}) copy-start(f32[4,32,1024]{2,1,0:T(8,128)} %get-tuple-element.5) | copy-start | bytes 1572868
